TPU v7x, 32 devices: a whole 2x2x4 slice. The times are simulated.
32 devices in a mesh: dp: 8 (over y, x, core), tensor: 4 (over z).
Axes of the slice: x: 2, y: 2, z: 4, core: 2. Of those that a mesh axis runs over, the one named last changes fastest.
Arguments:
- context: bfloat16 [7680, 6144], P('dp', 'tensor'), may hold values from -6 to 6
- out_grad: bfloat16 [7680, 32], P(('dp', 'tensor')), may hold values from -0.0625 to 0.0625
- owner_table: int32 [8], replicated, may hold values from 0 to 7, each once
- step_count: int32 [1], replicated, may hold values from 1 to 19
- master: float32 [8, 4, 6144], P('dp', None, 'tensor'), may hold values from -0.3125 to 0.3125
- first_moment: float32 [8, 4, 6144], P('dp', None, 'tensor'), may hold values from -6 to 6
- second_moment: float32 [8, 4, 6144], P('dp', None, 'tensor'), may hold values from 0.1 to 4
Outputs:
- new_master: float32 [8, 4, 6144], P('dp', None, 'tensor')
- new_first: float32 [8, 4, 6144], P('dp', None, 'tensor')
- new_second: float32 [8, 4, 6144], P('dp', None, 'tensor')
- new_weight: bfloat16 [32, 6144], P(None, 'tensor')
Inputs may be any that keep to these rules, and one draw needn't show every extreme that they name: `owner_table`: each state row holds exactly one bucket.
All inputs are finite; a program needn't handle non-finite values.
Results may differ from a plain program's by a relative error of at most 0.0004.
Values may be sent and summed in bfloat16 or wider, within the bound.
A program may use at most 64 MiB of HBM per device.

v0:
```python
import math

import jax
import jax.numpy as jnp
from jax import lax
from jax.sharding import PartitionSpec as P


def shards(context, out_grad, owner_table, step_count, master, first_moment, second_moment):
    buckets = owner_table.shape[0]
    per_dev = master.shape[0]
    width = master.shape[1]
    rows_dev = context.shape[1]
    all_tokens = lax.all_gather(out_grad, "tensor", axis=0, tiled=True)
    order = (
        jnp.zeros((buckets,), jnp.int32).at[owner_table].set(jnp.arange(buckets, dtype=jnp.int32))
    )
    first_row = lax.axis_index("dp") * per_dev
    own_ids = lax.dynamic_slice_in_dim(order, first_row, per_dev)
    product = lax.dot_general(
        all_tokens, context, (((0,), (0,)), ((), ())), preferred_element_type=jnp.float32
    )
    total = lax.psum(product.reshape(buckets, width, rows_dev), "dp")
    owned = jnp.take(total, own_ids, axis=0)
    new_first = 0.9 * first_moment + 0.1 * owned
    new_second = 0.95 * second_moment + 0.05 * owned * owned
    steps = step_count[0].astype(jnp.float32)
    corr_one = 1.0 - jnp.exp(steps * math.log(0.9))
    corr_two = 1.0 - jnp.exp(steps * math.log(0.95))
    update = new_first / corr_one / (jnp.sqrt(new_second / corr_two) + 1e-08)
    new_master = master - 0.01 * (update + 0.01 * master)
    fresh = new_master.astype(jnp.bfloat16)
    gathered = lax.all_gather(fresh, "dp", axis=0, tiled=True)
    new_weight = jnp.take(gathered, owner_table, axis=0).reshape(buckets * width, rows_dev)
    return (new_master, new_first, new_second, new_weight)


def solution(mesh):
    placed = (
        P("dp", "tensor"),
        P(("dp", "tensor"), None),
        P(),
        P(),
        P("dp", None, "tensor"),
        P("dp", None, "tensor"),
        P("dp", None, "tensor"),
    )
    return jax.shard_map(
        shards,
        mesh=mesh,
        in_specs=placed,
        out_specs=(
            P("dp", None, "tensor"),
            P("dp", None, "tensor"),
            P("dp", None, "tensor"),
            P(None, "tensor"),
        ),
        check_vma=False,
    )
```

profile of v0, /device:TPU:0, one launch (start us, length us, event | category | flops | bytes accessed | tf_op | source)
XLA Modules:
  0.0 96.9 jit_solution(5082387477488710111)
XLA Ops:
  7.2 0.0 copy-start
  7.2 0.0 copy-start.4
  7.2 0.0 copy-start.1
  7.2 0.0 copy-start.2
  7.2 0.0 copy-start.3
  7.2 0.0 all-reduce.2.cloned.1.call-start
  7.3 15.2 %all-gather = bf16[4,240,32]{1,2,0:T(8,128)(2,1)S(1)} all-gather(bf16[1,240,32]{1,2,0:T(8,128)(2,1)} %bitcast.9), channel_id=1, replica_groups=mesh['dp'=8,'tensor'=4] {'tensor'}, dimensions={0}, use_global_device_ids=true | all-gather | bytes 76800 | tf_op jit(solution)/shard_map/all_gather | solution.py:14
  22.5 0.1 copy.12
  22.6 0.1 reshape.101
  22.7 0.0 copy-done
  22.7 0.6 fusion.5
  23.3 0.7 reshape.53
  24.0 0.0 all-reduce.2.cloned.1.call-update
  24.1 0.0 copy-done.4
  24.9 0.6 scatter_custom_fusion
  25.5 0.6 dynamic_slice.3
  28.0 0.1 broadcast_in_dim.33
  28.1 0.1 broadcast_in_dim.34
  28.2 50.5 %all-reduce.2.cloned.1.call-done = f32[8,4,1536]{2,1,0:T(4,128)} async-done(((f32[8,4,1536]{2,1,0:T(4,128)}), f32[8,4,1536]{2,1,0:T(4,128)}) %all-reduce.2.cloned.1.call-update) | async-done | bytes 196624 | tf_op jit(solution)/shard_map/psum | solution.py:23
  78.7 0.0 copy-done.1
  78.7 0.0 copy-done.2
  78.7 0.0 copy-done.3
  78.7 1.4 %fusion.3 = (bf16[1,4,1536]{2,1,0:T(4,128)(2,1)S(1)}, f32[1,4,1536]{2,1,0:T(4,128)}, f32[1,4,1536]{2,1,0:T(4,128)}, f32[1,4,1536]{2,1,0:T(4,128)}) fusion(f32[1,4,1536]{2,1,0:T(4,128)S(1)} %copy-done.1, f32[]{:T(128)} %bitcast.4, f32[]{:T(128)} %bitcast.3, f32[8,4,1536]{2,1,0:T(4,128)} %all-reduce.2.cloned.1.call-done, s32[]{:T(128)} %bitcast.2, pred[]{:T(512)} %bitcast, ...), kind=kLoop, calls=%fused_computation.13 | loop fusion | flops 104448 | bytes 184333 | tf_op jit(solution)/shard_map/convert_element_type | solution.py:32
  80.1 8.5 %all_gather.7 = bf16[8,4,1536]{2,1,0:T(4,128)(2,1)S(1)} all-gather(bf16[1,4,1536]{2,1,0:T(4,128)(2,1)S(1)} %get-tuple-element.15), channel_id=1, replica_groups=mesh['dp'=8,'tensor'=4] {'dp'}, dimensions={0}, use_global_device_ids=true | all-gather | bytes 110592 | tf_op jit(solution)/shard_map/all_gather | solution.py:33
  88.6 0.6 gather_fusion
  89.3 0.7 broadcast_select_fusion
  (5 shorter events, 0.0 us)
Async XLA Ops:
  7.2 15.5 %copy-start = (bf16[960,1536]{1,0:T(8,128)(2,1)S(1)}, bf16[960,1536]{1,0:T(8,128)(2,1)}, u32[]{:S(2)}) copy-start(bf16[960,1536]{1,0:T(8,128)(2,1)} %param.7) | copy-start | bytes 8847364
  7.2 16.9 %copy-start.4 = (s32[8]{0:T(128)S(1)}, s32[8]{0:T(128)}, u32[]{:S(2)}) copy-start(s32[8]{0:T(128)} %param.9) | copy-start | bytes 100
  7.2 71.5 %copy-start.1 = (f32[1,4,1536]{2,1,0:T(4,128)S(1)}, f32[1,4,1536]{2,1,0:T(4,128)}, u32[]{:S(2)}) copy-start(f32[1,4,1536]{2,1,0:T(4,128)} %param.11) | copy-start | bytes 73732
  7.2 71.5 %copy-start.2 = (f32[1,4,1536]{2,1,0:T(4,128)S(1)}, f32[1,4,1536]{2,1,0:T(4,128)}, u32[]{:S(2)}) copy-start(f32[1,4,1536]{2,1,0:T(4,128)} %param.13) | copy-start | bytes 73732
  7.2 71.5 %copy-start.3 = (f32[1,4,1536]{2,1,0:T(4,128)S(1)}, f32[1,4,1536]{2,1,0:T(4,128)}, u32[]{:S(2)}) copy-start(f32[1,4,1536]{2,1,0:T(4,128)} %param.12) | copy-start | bytes 73732
  7.2 71.5 %all-reduce.2.cloned.1.call-start = ((), (), s32[]{:S(2)}) async-start(), calls=%async_computation | async-start | bytes 393216 | tf_op jit(solution)/shard_map/psum | solution.py:23
Sparse Core Ops, SparseCore 0:
  24.2 54.4 all-reduce.1
where the time goes:
time: 97.1 us; the launch traced here: 96.9 us
  waiting for transfers between devices  50.5 us (52%)
  blocking collectives  23.8 us (25%)
  between operations  16.8 us (17%)
  local copies, waits for them, and re-layouts  2.95 us (3%)
  other arithmetic  2.14 us (2%)
    psum x1, waiting for transfers between devices, shards(): total = lax.psum(product.reshape(buckets, width, rows_dev), 'dp')  50.5 us
    all_gather x1, blocking collectives, shards(): all_tokens = lax.all_gather(out_grad, 'tensor', axis=0, tiled=True)  15.2 us
    all_gather x1, blocking collectives, shards(): gathered = lax.all_gather(fresh, 'dp', axis=0, tiled=True)  8.53 us
  transfers between devices with their start and end apart: 1, of which 1 were waited for; matrix products, arithmetic and copies ran while one was open for 1% of the time, Pallas kernels for 0%

commit v1 on v0

v1 whole, which is shorter than its diff:
```python
import functools
import math

import jax
import jax.numpy as jnp
from jax import lax
from jax.experimental import pallas as pl
from jax.experimental.pallas import tpu as pltpu
from jax.sharding import PartitionSpec as P

F32 = jnp.float32
BF16 = jnp.bfloat16


def each(low, high, body):
    if high - low <= 16:
        for at in range(low, high):
            body(at)
    else:
        lax.fori_loop(low, high, lambda at, none: (body(at), none)[1], None)


def kernel(
    owners, ranks, buckets, width,
    table, step, og_hbm, ctx_hbm, master_hbm, first_hbm, second_hbm,
    out_master, out_first, out_second, out_weight,
    og_own, og_all, ctx, acc, stage, parts, state, fresh, rows, weight,
    og_own_sem, ctx_sem, state_sem, out_sem,
    og_send, og_recv, part_send, part_recv, row_send, row_recv,
):
    me = lax.axis_index("dp")
    rank = lax.axis_index("tensor")
    window, tokens = og_own.shape
    columns = ctx.shape[2]
    groups = rows.shape[1] // width
    span = columns // groups

    barrier = pltpu.get_barrier_semaphore()

    def greet_rank(k):
        pl.semaphore_signal(barrier, inc=1, device_id={"tensor": lax.rem(rank + k, ranks)})

    def greet_owner(k):
        pl.semaphore_signal(barrier, inc=1, device_id={"dp": lax.rem(me + k, owners)})

    each(1, ranks, greet_rank)
    each(1, owners, greet_owner)

    own_copy = pltpu.make_async_copy(og_hbm, og_own, og_own_sem)
    own_copy.start()

    def ctx_copy(k):
        at = lax.rem(rank + k, ranks)
        first = pl.multiple_of(at * tokens, 16)
        return pltpu.make_async_copy(
            ctx_hbm.at[pl.ds(first, tokens), :], ctx.at[at], ctx_sem.at[at]
        )

    for k in range(ranks):
        ctx_copy(k).start()
    state_copies = [
        pltpu.make_async_copy(source.at[0], state.at[i], state_sem.at[i])
        for i, source in enumerate((master_hbm, first_hbm, second_hbm))
    ]
    for copy in state_copies:
        copy.start()

    lane_bucket = lax.broadcasted_iota(jnp.int32, (1, window), 1) // width
    owner_of = jnp.zeros((1, window), jnp.int32)
    for b in range(buckets):
        owner_of = jnp.where(lane_bucket == b, table[b], owner_of)
    down = lax.broadcasted_iota(jnp.int32, (window, window), 0)
    across = lax.broadcasted_iota(jnp.int32, (window, window), 1)
    chosen = jnp.logical_and(owner_of == down // width, down % width == across % width)
    pick = jnp.where(chosen, 1.0, 0.0).astype(BF16)

    own_copy.wait()
    og_all[rank] = jnp.dot(pick, og_own[...], preferred_element_type=F32).astype(BF16)

    pl.semaphore_wait(barrier, ranks + owners - 2)

    def og_copy(k):
        peer = lax.rem(rank + k, ranks)
        return pltpu.make_async_remote_copy(
            src_ref=og_all.at[rank],
            dst_ref=og_all.at[rank],
            send_sem=og_send.at[k],
            recv_sem=og_recv.at[k],
            device_id={"tensor": peer},
        )

    def og_arrival(k):
        source = lax.rem(rank + ranks - k, ranks)
        return pltpu.make_async_remote_copy(
            src_ref=og_all.at[source],
            dst_ref=og_all.at[source],
            send_sem=og_send.at[k],
            recv_sem=og_recv.at[k],
            device_id={"tensor": source},
        )

    for k in range(1, ranks):
        og_copy(k).start()

    block = min(window, 8 * width)
    for i in range(ranks):
        at = lax.rem(rank + ranks - i, ranks)
        if i:
            og_arrival(i).wait_recv()
        ctx_copy((ranks - i) % ranks).wait()

        def multiply(m, i=i, at=at):
            here = pl.ds(m * block, block)
            value = jnp.dot(og_all[at, here, :], ctx[at], preferred_element_type=F32)
            if i:
                value = acc[here, :] + value
            if i < ranks - 1:
                acc[here, :] = value
            else:
                for j in range(block // width):
                    stage[m * (block // width) + j] = value[j * width:(j + 1) * width, :]

        each(0, window // block, multiply)

    def part_copy(k):
        peer = lax.rem(me + k, owners)
        return pltpu.make_async_remote_copy(
            src_ref=stage.at[peer],
            dst_ref=parts.at[k],
            send_sem=part_send.at[k],
            recv_sem=part_recv.at[k],
            device_id={"dp": peer},
        )

    each(1, owners, lambda k: part_copy(k).start())

    steps = jnp.full((1, columns), step[0], jnp.int32).astype(F32)
    corr_one = 1.0 - jnp.exp(steps * math.log(0.9))
    corr_two = 1.0 - jnp.exp(steps * math.log(0.95))
    for copy in state_copies:
        copy.wait()

    acc_own = acc.at[pl.ds(0, width), :]
    acc_own[...] = stage[me]

    def take(k):
        part_copy(k).wait_recv()
        acc_own[...] += parts[k]

    each(1, owners, take)
    owned = acc_own[...]
    master = state[0]
    new_first = 0.9 * state[1] + 0.1 * owned
    new_second = 0.95 * state[2] + 0.05 * owned * owned
    update = new_first / corr_one / (jnp.sqrt(new_second / corr_two) + 1e-08)
    new_master = master - 0.01 * (update + 0.01 * master)
    packed = jnp.concatenate(
        [new_master[:, g * span:(g + 1) * span] for g in range(groups)], axis=0
    )
    rows[me] = packed.astype(BF16)

    def row_copy(k):
        return pltpu.make_async_remote_copy(
            src_ref=rows.at[me],
            dst_ref=rows.at[me],
            send_sem=row_send.at[k],
            recv_sem=row_recv.at[k],
            device_id={"dp": lax.rem(me + k, owners)},
        )

    def row_arrival(k):
        source = lax.rem(me + owners - k, owners)
        return pltpu.make_async_remote_copy(
            src_ref=rows.at[source],
            dst_ref=rows.at[source],
            send_sem=row_send.at[k],
            recv_sem=row_recv.at[k],
            device_id={"dp": source},
        )

    each(1, owners, lambda k: row_copy(k).start())
    fresh[0] = new_master
    fresh[1] = new_first
    fresh[2] = new_second
    out_copies = [
        pltpu.make_async_copy(fresh.at[i], target.at[0], out_sem.at[i])
        for i, target in enumerate((out_master, out_first, out_second))
    ]
    for copy in out_copies:
        copy.start()

    each(1, owners, lambda k: row_arrival(k).wait_recv())

    def assemble(q):
        blocks = [rows[table[q * groups + j]].astype(F32) for j in range(groups)]
        for g in range(groups):
            piece = jnp.concatenate(
                [b[g * width:(g + 1) * width, :] for b in blocks], axis=0
            )
            weight[pl.ds(pl.multiple_of(q * groups * width, 16), groups * width),
                   g * span:(g + 1) * span] = piece.astype(BF16)

    each(0, buckets // groups, assemble)
    weight_copy = pltpu.make_async_copy(weight, out_weight, out_sem.at[3])
    weight_copy.start()

    for k in range(1, ranks):
        og_copy(k).wait_send()
    each(1, owners, lambda k: part_copy(k).wait_send())
    each(1, owners, lambda k: row_copy(k).wait_send())
    for copy in out_copies:
        copy.wait()
    weight_copy.wait()


def shards(owners, ranks, context, out_grad, owner_table, step_count, master, first, second):
    buckets = owner_table.shape[0]
    width = master.shape[1]
    tokens, window = out_grad.shape
    columns = context.shape[1]
    groups = 16 // width
    state_shape = jax.ShapeDtypeStruct(master.shape, F32)
    hbm = pl.BlockSpec(memory_space=pltpu.HBM)
    smem = pl.BlockSpec(memory_space=pltpu.SMEM)
    dma = pltpu.SemaphoreType.DMA
    return pl.pallas_call(
        functools.partial(kernel, owners, ranks, buckets, width),
        out_shape=(
            state_shape,
            state_shape,
            state_shape,
            jax.ShapeDtypeStruct((window, columns), BF16),
        ),
        in_specs=[smem, smem] + [hbm] * 5,
        out_specs=(hbm,) * 4,
        scratch_shapes=[
            pltpu.VMEM((window, tokens), BF16),
            pltpu.VMEM((ranks, window, tokens), BF16),
            pltpu.VMEM((ranks, tokens, columns), BF16),
            pltpu.VMEM((window, columns), F32),
            pltpu.VMEM((owners, width, columns), F32),
            pltpu.VMEM((owners, width, columns), F32),
            pltpu.VMEM((3, width, columns), F32),
            pltpu.VMEM((3, width, columns), F32),
            pltpu.VMEM((owners, groups * width, columns // groups), BF16),
            pltpu.VMEM((window, columns), BF16),
            dma, dma((ranks,)), dma((3,)), dma((4,)),
            dma((ranks,)), dma((ranks,)),
            dma((owners,)), dma((owners,)),
            dma((owners,)), dma((owners,)),
        ],
        compiler_params=pltpu.CompilerParams(
            collective_id=0, has_side_effects=True, vmem_limit_bytes=40 * 1024 * 1024
        ),
        cost_estimate=pl.CostEstimate(
            flops=2 * window * columns * tokens * ranks,
            bytes_accessed=2 * ranks * tokens * columns,
            transcendentals=0,
        ),
    )(owner_table, step_count, out_grad.T, context, master, first, second)


def solution(mesh):
    placed = (
        P("dp", "tensor"),
        P(("dp", "tensor"), None),
        P(),
        P(),
        P("dp", None, "tensor"),
        P("dp", None, "tensor"),
        P("dp", None, "tensor"),
    )
    return jax.shard_map(
        functools.partial(shards, mesh.shape["dp"], mesh.shape["tensor"]),
        mesh=mesh,
        in_specs=placed,
        out_specs=(
            P("dp", None, "tensor"),
            P("dp", None, "tensor"),
            P("dp", None, "tensor"),
            P(None, "tensor"),
        ),
        check_vma=False,
    )
```

time: 97.1 us -> 27.6 us (0.28)
  waiting for transfers between devices: 50.5 us -> 0 us
  blocking collectives: 23.8 us -> 0 us
  Pallas kernels: 0 us -> 18.1 us
  between operations: 16.8 us -> 1.3 us
  local copies, waits for them, and re-layouts: 2.95 us -> 7.87 us
  other arithmetic: 2.14 us -> 0 us
    psum x1 -> x0, waiting for transfers between devices: 50.5 us -> none  [shards(): total = lax.psum(product.reshape(buckets, width, rows_dev), 'dp')]
    all_gather x2 -> x0, blocking collectives: 23.8 us -> none  [the longest x1 15.2 us: shards(): all_tokens = lax.all_gather(out_grad, 'tensor', axis=0, tiled=True)]
    pallas_call x0 -> x1, Pallas kernels: none -> 18.1 us  [shards(): pl.pallas_call(functools.partial(kernel, owners, ranks, buckets, width),...]
    unnamed x11 -> x16, local copies, waits for them, and re-layouts: 0.14 us -> 7.87 us
    convert_element_type x1 -> x0, other arithmetic: 1.4 us -> none  [shards(): fresh = new_master.astype(jnp.bfloat16)]
  transfers between devices with their start and end apart: 1 -> 0, of which waited for: 1 -> 0; matrix products, arithmetic and copies ran while one was open for 1% -> 0% of each run, Pallas kernels for 0% -> 0%
where the time goes in v1:
time: 27.6 us; the launch traced here: 27.2 us
  Pallas kernels  18.1 us (66%)
  local copies, waits for them, and re-layouts  7.87 us (29%)
  between operations  1.3 us (5%)
    pallas_call x1, Pallas kernels, shards(): pl.pallas_call(functools.partial(kernel, owners, ranks, buckets, width),...  18.1 us
    unnamed x16, local copies, waits for them, and re-layouts  7.87 us

profile of v1, /device:TPU:0, one launch (start us, length us, event | category | flops | bytes accessed | tf_op | source)
XLA Modules:
  0.0 27.2 jit_solution(13705225051434555464)
XLA Ops:
  1.3 0.0 copy-start
  1.3 1.8 %copy-done = bf16[960,1536]{1,0:T(8,128)(2,1)S(1)} copy-done((bf16[960,1536]{1,0:T(8,128)(2,1)S(1)}, bf16[960,1536]{1,0:T(8,128)(2,1)}, u32[]{:S(2)}) %copy-start) | copy-done | bytes 2949144
  3.1 0.0 copy-start.1
  3.1 0.7 %copy-done.1 = f32[1,4,1536]{2,1,0:T(4,128)S(1)} copy-done((f32[1,4,1536]{2,1,0:T(4,128)S(1)}, f32[1,4,1536]{2,1,0:T(4,128)}, u32[]{:S(2)}) %copy-start.1) | copy-done | bytes 24600
  3.9 0.0 copy-start.2
  3.9 0.7 %copy-done.2 = f32[1,4,1536]{2,1,0:T(4,128)S(1)} copy-done((f32[1,4,1536]{2,1,0:T(4,128)S(1)}, f32[1,4,1536]{2,1,0:T(4,128)}, u32[]{:S(2)}) %copy-start.2) | copy-done | bytes 24600
  4.6 0.0 copy-start.3
  4.6 0.7 %copy-done.3 = f32[1,4,1536]{2,1,0:T(4,128)S(1)} copy-done((f32[1,4,1536]{2,1,0:T(4,128)S(1)}, f32[1,4,1536]{2,1,0:T(4,128)}, u32[]{:S(2)}) %copy-start.3) | copy-done | bytes 24600
  5.3 0.0 copy-start.4
  5.3 0.7 %copy-done.4 = bf16[240,32]{0,1:T(8,128)(2,1)S(1)} copy-done((bf16[240,32]{0,1:T(8,128)(2,1)S(1)}, bf16[240,32]{0,1:T(8,128)(2,1)}, u32[]{:S(2)}) %copy-start.4) | copy-done | bytes 15384
  6.0 0.0 copy-start.5
  6.0 0.7 %copy-done.5 = s32[8]{0:T(128)S(1)} copy-done((s32[8]{0:T(128)S(1)}, s32[8]{0:T(128)}, u32[]{:S(2)}) %copy-start.5) | copy-done | bytes 56
  6.7 18.1 %shard_map.102 = (f32[1,4,1536]{2,1,0:T(4,128)S(1)}, f32[1,4,1536]{2,1,0:T(4,128)S(1)}, f32[1,4,1536]{2,1,0:T(4,128)S(1)}, bf16[32,1536]{1,0:T(8,128)(2,1)S(1)}) custom-call(s32[8]{0:T(128)S(1)} %copy-done.5, s32[1]{0:T(128)S(6)} %copy.15.step, bf16[32,240]{1,0:T(8,128)(2,1)S(1)} %bitcast.1, bf16[960,1536]{1,0:T(8,128)(2,1)S(1)} %copy-done, ...), custom_call_target="tpu_custom_call" | custom-call | flops 94371840 | bytes 2949120 | tf_op jit(solution)/shard_map/pallas_call | solution.py:226
  24.8 0.6 %copy.16 = f32[1,4,1536]{2,1,0:T(4,128)} copy(f32[1,4,1536]{2,1,0:T(4,128)S(1)} %get-tuple-element.8) | data formatting | bytes 49152
  25.4 0.6 %copy.17 = f32[1,4,1536]{2,1,0:T(4,128)} copy(f32[1,4,1536]{2,1,0:T(4,128)S(1)} %get-tuple-element.9) | data formatting | bytes 49152
  26.0 0.6 %copy.18 = f32[1,4,1536]{2,1,0:T(4,128)} copy(f32[1,4,1536]{2,1,0:T(4,128)S(1)} %get-tuple-element.10) | data formatting | bytes 49152
  26.6 0.6 %copy.19 = bf16[32,1536]{1,0:T(8,128)(2,1)} copy(bf16[32,1536]{1,0:T(8,128)(2,1)S(1)} %get-tuple-element.11) | data formatting | bytes 196608
Async XLA Ops:
  1.3 1.8 %copy-start = (bf16[960,1536]{1,0:T(8,128)(2,1)S(1)}, bf16[960,1536]{1,0:T(8,128)(2,1)}, u32[]{:S(2)}) copy-start(bf16[960,1536]{1,0:T(8,128)(2,1)} %ctx_hbm.1) | copy-start | bytes 8847364
  3.1 0.7 %copy-start.1 = (f32[1,4,1536]{2,1,0:T(4,128)S(1)}, f32[1,4,1536]{2,1,0:T(4,128)}, u32[]{:S(2)}) copy-start(f32[1,4,1536]{2,1,0:T(4,128)} %master_hbm.1) | copy-start | bytes 73732
  3.9 0.7 %copy-start.2 = (f32[1,4,1536]{2,1,0:T(4,128)S(1)}, f32[1,4,1536]{2,1,0:T(4,128)}, u32[]{:S(2)}) copy-start(f32[1,4,1536]{2,1,0:T(4,128)} %first_hbm.1) | copy-start | bytes 73732
  4.6 0.7 %copy-start.3 = (f32[1,4,1536]{2,1,0:T(4,128)S(1)}, f32[1,4,1536]{2,1,0:T(4,128)}, u32[]{:S(2)}) copy-start(f32[1,4,1536]{2,1,0:T(4,128)} %second_hbm.1) | copy-start | bytes 73732
  5.3 0.7 %copy-start.4 = (bf16[240,32]{0,1:T(8,128)(2,1)S(1)}, bf16[240,32]{0,1:T(8,128)(2,1)}, u32[]{:S(2)}) copy-start(bf16[240,32]{0,1:T(8,128)(2,1)} %param.8) | copy-start | bytes 46084
  6.0 0.7 %copy-start.5 = (s32[8]{0:T(128)S(1)}, s32[8]{0:T(128)}, u32[]{:S(2)}) copy-start(s32[8]{0:T(128)} %table.1) | copy-start | bytes 100

commit v2 on v1

--- a/solution.py
+++ b/solution.py
@@ -22,15 +22,15 @@
 
 def kernel(
     owners, ranks, buckets, width,
-    table, step, og_hbm, ctx_hbm, master_hbm, first_hbm, second_hbm,
-    out_master, out_first, out_second, out_weight,
-    og_own, og_all, ctx, acc, stage, parts, state, fresh, rows, weight,
-    og_own_sem, ctx_sem, state_sem, out_sem,
+    table_hbm, step, og_hbm, ctx_hbm, master_hbm, first_hbm, second_hbm,
+    out_master, out_first, out_second, rows,
+    table, table_sem, og_all, ctx, acc, product, stage, parts, state,
+    og_own_sem, ctx_sem, state_sem,
     og_send, og_recv, part_send, part_recv, row_send, row_recv,
 ):
     me = lax.axis_index("dp")
     rank = lax.axis_index("tensor")
-    window, tokens = og_own.shape
+    window, tokens = og_hbm.shape
     columns = ctx.shape[2]
     groups = rows.shape[1] // width
     span = columns // groups
@@ -46,7 +46,9 @@
     each(1, ranks, greet_rank)
     each(1, owners, greet_owner)
 
-    own_copy = pltpu.make_async_copy(og_hbm, og_own, og_own_sem)
+    table_copy = pltpu.make_async_copy(table_hbm, table, table_sem)
+    table_copy.start()
+    own_copy = pltpu.make_async_copy(og_hbm, og_all.at[rank], og_own_sem)
     own_copy.start()
 
     def ctx_copy(k):
@@ -65,18 +67,21 @@
     for copy in state_copies:
         copy.start()
 
-    lane_bucket = lax.broadcasted_iota(jnp.int32, (1, window), 1) // width
-    owner_of = jnp.zeros((1, window), jnp.int32)
-    for b in range(buckets):
-        owner_of = jnp.where(lane_bucket == b, table[b], owner_of)
-    down = lax.broadcasted_iota(jnp.int32, (window, window), 0)
-    across = lax.broadcasted_iota(jnp.int32, (window, window), 1)
-    chosen = jnp.logical_and(owner_of == down // width, down % width == across % width)
-    pick = jnp.where(chosen, 1.0, 0.0).astype(BF16)
+    def bucket_of(r):
+        def check(b, found):
+            return jnp.where(table[b] == r, b, found)
+
+        if buckets > 16:
+            return lax.fori_loop(0, buckets, check, 0)
+        found = 0
+        for b in range(buckets):
+            found = check(b, found)
+        return found
+
+    table_copy.wait()
+    ready = [bucket_of(r) for r in range(buckets)] if buckets <= 16 else None
 
     own_copy.wait()
-    og_all[rank] = jnp.dot(pick, og_own[...], preferred_element_type=F32).astype(BF16)
-
     pl.semaphore_wait(barrier, ranks + owners - 2)
 
     def og_copy(k):
@@ -118,9 +123,14 @@
                 acc[here, :] = value
             else:
                 for j in range(block // width):
-                    stage[m * (block // width) + j] = value[j * width:(j + 1) * width, :]
+                    product[m * (block // width) + j] = value[j * width:(j + 1) * width, :]
 
         each(0, window // block, multiply)
+
+    def place(r):
+        stage[r] = product[ready[r] if ready else bucket_of(r)]
+
+    each(0, buckets, place)
 
     def part_copy(k):
         peer = lax.rem(me + k, owners)
@@ -154,10 +164,10 @@
     new_second = 0.95 * state[2] + 0.05 * owned * owned
     update = new_first / corr_one / (jnp.sqrt(new_second / corr_two) + 1e-08)
     new_master = master - 0.01 * (update + 0.01 * master)
-    packed = jnp.concatenate(
+    joined = jnp.concatenate(
         [new_master[:, g * span:(g + 1) * span] for g in range(groups)], axis=0
     )
-    rows[me] = packed.astype(BF16)
+    rows[me] = joined.astype(BF16)
 
     def row_copy(k):
         return pltpu.make_async_remote_copy(
@@ -179,17 +189,32 @@
         )
 
     each(1, owners, lambda k: row_copy(k).start())
-    fresh[0] = new_master
-    fresh[1] = new_first
-    fresh[2] = new_second
-    out_copies = [
-        pltpu.make_async_copy(fresh.at[i], target.at[0], out_sem.at[i])
-        for i, target in enumerate((out_master, out_first, out_second))
+    out_master[0] = new_master
+    out_first[0] = new_first
+    out_second[0] = new_second
+
+    each(1, owners, lambda k: row_arrival(k).wait_recv())
+
+    for k in range(1, ranks):
+        og_copy(k).wait_send()
+    each(1, owners, lambda k: part_copy(k).wait_send())
+    each(1, owners, lambda k: row_copy(k).wait_send())
+
+
+def finish_kernel(
+    buckets, width, table, master, first, second, rows,
+    out_master, out_first, out_second, out_weight, weight, out_sem,
+):
+    groups = rows.shape[1] // width
+    span = rows.shape[2]
+    copies = [
+        pltpu.make_async_copy(source, target, out_sem.at[i])
+        for i, (source, target) in enumerate(
+            ((master, out_master), (first, out_first), (second, out_second))
+        )
     ]
-    for copy in out_copies:
+    for copy in copies:
         copy.start()
-
-    each(1, owners, lambda k: row_arrival(k).wait_recv())
 
     def assemble(q):
         blocks = [rows[table[q * groups + j]].astype(F32) for j in range(groups)]
@@ -197,18 +222,13 @@
             piece = jnp.concatenate(
                 [b[g * width:(g + 1) * width, :] for b in blocks], axis=0
             )
-            weight[pl.ds(pl.multiple_of(q * groups * width, 16), groups * width),
-                   g * span:(g + 1) * span] = piece.astype(BF16)
+            here = pl.ds(pl.multiple_of(q * groups * width, 16), groups * width)
+            weight[here, g * span:(g + 1) * span] = piece.astype(BF16)
 
     each(0, buckets // groups, assemble)
     weight_copy = pltpu.make_async_copy(weight, out_weight, out_sem.at[3])
     weight_copy.start()
-
-    for k in range(1, ranks):
-        og_copy(k).wait_send()
-    each(1, owners, lambda k: part_copy(k).wait_send())
-    each(1, owners, lambda k: row_copy(k).wait_send())
-    for copy in out_copies:
+    for copy in copies:
         copy.wait()
     weight_copy.wait()
 
@@ -223,34 +243,34 @@
     hbm = pl.BlockSpec(memory_space=pltpu.HBM)
     smem = pl.BlockSpec(memory_space=pltpu.SMEM)
     dma = pltpu.SemaphoreType.DMA
-    return pl.pallas_call(
+    weight_shape = jax.ShapeDtypeStruct((window, columns), BF16)
+    new_master, new_first, new_second, rows = pl.pallas_call(
         functools.partial(kernel, owners, ranks, buckets, width),
         out_shape=(
-            state_shape,
-            state_shape,
-            state_shape,
-            jax.ShapeDtypeStruct((window, columns), BF16),
+            pltpu.VMEM(master.shape, F32),
+            pltpu.VMEM(master.shape, F32),
+            pltpu.VMEM(master.shape, F32),
+            pltpu.VMEM((owners, groups * width, columns // groups), BF16),
         ),
-        in_specs=[smem, smem] + [hbm] * 5,
-        out_specs=(hbm,) * 4,
+        in_specs=[hbm, smem] + [hbm] * 5,
+        out_specs=(pl.BlockSpec(memory_space=pltpu.VMEM),) * 4,
         scratch_shapes=[
-            pltpu.VMEM((window, tokens), BF16),
+            pltpu.SMEM((buckets,), jnp.int32),
+            dma,
             pltpu.VMEM((ranks, window, tokens), BF16),
             pltpu.VMEM((ranks, tokens, columns), BF16),
             pltpu.VMEM((window, columns), F32),
+            pltpu.VMEM((buckets, width, columns), F32),
             pltpu.VMEM((owners, width, columns), F32),
             pltpu.VMEM((owners, width, columns), F32),
             pltpu.VMEM((3, width, columns), F32),
-            pltpu.VMEM((3, width, columns), F32),
-            pltpu.VMEM((owners, groups * width, columns // groups), BF16),
-            pltpu.VMEM((window, columns), BF16),
-            dma, dma((ranks,)), dma((3,)), dma((4,)),
+            dma, dma((ranks,)), dma((3,)),
             dma((ranks,)), dma((ranks,)),
             dma((owners,)), dma((owners,)),
             dma((owners,)), dma((owners,)),
         ],
         compiler_params=pltpu.CompilerParams(
-            collective_id=0, has_side_effects=True, vmem_limit_bytes=40 * 1024 * 1024
+            collective_id=0, has_side_effects=True, vmem_limit_bytes=56 * 1024 * 1024
         ),
         cost_estimate=pl.CostEstimate(
             flops=2 * window * columns * tokens * ranks,
@@ -258,6 +278,14 @@
             transcendentals=0,
         ),
     )(owner_table, step_count, out_grad.T, context, master, first, second)
+    return pl.pallas_call(
+        functools.partial(finish_kernel, buckets, width),
+        out_shape=(state_shape, state_shape, state_shape, weight_shape),
+        in_specs=[smem] + [hbm] * 3 + [pl.BlockSpec(memory_space=pltpu.VMEM)],
+        out_specs=(hbm,) * 4,
+        scratch_shapes=[pltpu.VMEM((window, columns), BF16), dma((4,))],
+        compiler_params=pltpu.CompilerParams(vmem_limit_bytes=16 * 1024 * 1024),
+    )(owner_table, new_master, new_first, new_second, rows)
 
 
 def solution(mesh):

time: 27.6 us -> 20.1 us (0.73)
  local copies, waits for them, and re-layouts: 7.87 us -> 0.01 us
  Pallas kernels: 18.1 us -> 18.6 us
    unnamed x16 -> x2, local copies, waits for them, and re-layouts: 7.87 us -> 0.01 us
    pallas_call x0 -> x1, Pallas kernels: none -> 1.25 us  [shards(): pl.pallas_call(functools.partial(finish_kernel, buckets, width), out_shap...]
    pallas_call x1, Pallas kernels: 18.1 us -> 17.3 us  [shards(): pl.pallas_call(functools.partial(kernel, owners, ranks, buckets, width),...]
where the time goes in v2:
time: 20.1 us; the launch traced here: 19.9 us
  Pallas kernels  18.6 us (93%)
  between operations  1.32 us (7%)
    pallas_call x1, Pallas kernels, shards(): pl.pallas_call(functools.partial(kernel, owners, ranks, buckets, width),...  17.3 us
    pallas_call x1, Pallas kernels, shards(): pl.pallas_call(functools.partial(finish_kernel, buckets, width), out_shap...  1.25 us

profile of v2, /device:TPU:0, one launch (start us, length us, event | category | flops | bytes accessed | tf_op | source)
XLA Modules:
  0.0 19.9 jit_solution(17199203257856283608)
XLA Ops:
  0.6 0.0 copy-start
  1.3 17.3 %shard_map.102 = (f32[1,4,1536]{2,1,0:T(4,128)S(1)}, f32[1,4,1536]{2,1,0:T(4,128)S(1)}, f32[1,4,1536]{2,1,0:T(4,128)S(1)}, bf16[8,16,384]{2,1,0:T(8,128)(2,1)S(1)}) custom-call(s32[8]{0:T(128)} %table.1, s32[1]{0:T(128)S(6)} %copy.11.step, bf16[32,240]{1,0:T(8,128)(2,1)} %bitcast.1, bf16[960,1536]{1,0:T(8,128)(2,1)} %ctx_hbm.1, f32[1,4,1536]{2,1,0:T(4,128)} %master_hbm.1, ...), custom_call_target="tpu_custom_call" | custom-call | flops 94371840 | bytes 2949120 | tf_op jit(solution)/shard_map/pallas_call | solution.py:247
  18.7 0.0 copy-done
  18.7 1.2 %shard_map.103 = (f32[1,4,1536]{2,1,0:T(4,128)}, f32[1,4,1536]{2,1,0:T(4,128)}, f32[1,4,1536]{2,1,0:T(4,128)}, bf16[32,1536]{1,0:T(8,128)(2,1)}) custom-call(s32[8]{0:T(128)S(1)} %copy-done, f32[1,4,1536]{2,1,0:T(4,128)S(1)} %get-tuple-element.8.master, f32[1,4,1536]{2,1,0:T(4,128)S(1)} %get-tuple-element.9.first, ...), custom_call_target="tpu_custom_call" | custom-call | tf_op jit(solution)/shard_map/pallas_call | solution.py:281
Async XLA Ops:
  0.6 18.0 %copy-start = (s32[8]{0:T(128)S(1)}, s32[8]{0:T(128)}, u32[]{:S(2)}) copy-start(s32[8]{0:T(128)} %table.1) | copy-start | bytes 100

commit v3 on v2

--- a/solution.py
+++ b/solution.py
@@ -18,6 +18,14 @@
             body(at)
     else:
         lax.fori_loop(low, high, lambda at, none: (body(at), none)[1], None)
+
+
+def flipped(at, k, size):
+    total, bit = 0, 1
+    while bit < size:
+        total = total + (at // bit + k // bit) % 2 * bit
+        bit *= 2
+    return total
 
 
 def kernel(
@@ -38,12 +46,12 @@
     barrier = pltpu.get_barrier_semaphore()
 
     def greet_rank(k):
-        pl.semaphore_signal(barrier, inc=1, device_id={"tensor": lax.rem(rank + k, ranks)})
+        pl.semaphore_signal(barrier, inc=1, device_id={"tensor": flipped(rank, k, ranks)})
 
     def greet_owner(k):
-        pl.semaphore_signal(barrier, inc=1, device_id={"dp": lax.rem(me + k, owners)})
-
-    each(1, ranks, greet_rank)
+        pl.semaphore_signal(barrier, inc=1, device_id={"dp": flipped(me, k, owners)})
+
+    each(1, ranks, lambda k: greet_rank(ranks - k))
     each(1, owners, greet_owner)
 
     table_copy = pltpu.make_async_copy(table_hbm, table, table_sem)
@@ -52,7 +60,7 @@
     own_copy.start()
 
     def ctx_copy(k):
-        at = lax.rem(rank + k, ranks)
+        at = flipped(rank, k, ranks)
         first = pl.multiple_of(at * tokens, 16)
         return pltpu.make_async_copy(
             ctx_hbm.at[pl.ds(first, tokens), :], ctx.at[at], ctx_sem.at[at]
@@ -85,7 +93,7 @@
     pl.semaphore_wait(barrier, ranks + owners - 2)
 
     def og_copy(k):
-        peer = lax.rem(rank + k, ranks)
+        peer = flipped(rank, k, ranks)
         return pltpu.make_async_remote_copy(
             src_ref=og_all.at[rank],
             dst_ref=og_all.at[rank],
@@ -95,7 +103,7 @@
         )
 
     def og_arrival(k):
-        source = lax.rem(rank + ranks - k, ranks)
+        source = flipped(rank, k, ranks)
         return pltpu.make_async_remote_copy(
             src_ref=og_all.at[source],
             dst_ref=og_all.at[source],
@@ -104,15 +112,15 @@
             device_id={"tensor": source},
         )
 
-    for k in range(1, ranks):
+    for k in range(ranks - 1, 0, -1):
         og_copy(k).start()
 
     block = min(window, 8 * width)
     for i in range(ranks):
-        at = lax.rem(rank + ranks - i, ranks)
+        at = flipped(rank, i, ranks)
         if i:
             og_arrival(i).wait_recv()
-        ctx_copy((ranks - i) % ranks).wait()
+        ctx_copy(i).wait()
 
         def multiply(m, i=i, at=at):
             here = pl.ds(m * block, block)
@@ -133,7 +141,7 @@
     each(0, buckets, place)
 
     def part_copy(k):
-        peer = lax.rem(me + k, owners)
+        peer = flipped(me, k, owners)
         return pltpu.make_async_remote_copy(
             src_ref=stage.at[peer],
             dst_ref=parts.at[k],
@@ -142,7 +150,7 @@
             device_id={"dp": peer},
         )
 
-    each(1, owners, lambda k: part_copy(k).start())
+    each(1, owners, lambda k: part_copy(owners - k).start())
 
     steps = jnp.full((1, columns), step[0], jnp.int32).astype(F32)
     corr_one = 1.0 - jnp.exp(steps * math.log(0.9))
@@ -175,11 +183,11 @@
             dst_ref=rows.at[me],
             send_sem=row_send.at[k],
             recv_sem=row_recv.at[k],
-            device_id={"dp": lax.rem(me + k, owners)},
+            device_id={"dp": flipped(me, k, owners)},
         )
 
     def row_arrival(k):
-        source = lax.rem(me + owners - k, owners)
+        source = flipped(me, k, owners)
         return pltpu.make_async_remote_copy(
             src_ref=rows.at[source],
             dst_ref=rows.at[source],
@@ -188,7 +196,7 @@
             device_id={"dp": source},
         )
 
-    each(1, owners, lambda k: row_copy(k).start())
+    each(1, owners, lambda k: row_copy(owners - k).start())
     out_master[0] = new_master
     out_first[0] = new_first
     out_second[0] = new_second

time: 20.1 us -> 19.7 us (0.980)
  Pallas kernels: 18.6 us -> 18.2 us
    pallas_call x1, Pallas kernels: 17.3 us -> 16.9 us  [shards(): pl.pallas_call(functools.partial(kernel, owners, ranks, buckets, width),...]
where the time goes in v3:
time: 19.7 us; the launch traced here: 19.5 us
  Pallas kernels  18.2 us (92%)
  between operations  1.32 us (7%)
    pallas_call x1, Pallas kernels, shards(): pl.pallas_call(functools.partial(kernel, owners, ranks, buckets, width),...  16.9 us
    pallas_call x1, Pallas kernels, shards(): pl.pallas_call(functools.partial(finish_kernel, buckets, width), out_shap...  1.25 us

profile of v3, /device:TPU:0, one launch (start us, length us, event | category | flops | bytes accessed | tf_op | source)
XLA Modules:
  0.0 19.5 jit_solution(5998439888692686710)
XLA Ops:
  0.6 0.0 copy-start
  1.3 16.9 %shard_map.102 = (f32[1,4,1536]{2,1,0:T(4,128)S(1)}, f32[1,4,1536]{2,1,0:T(4,128)S(1)}, f32[1,4,1536]{2,1,0:T(4,128)S(1)}, bf16[8,16,384]{2,1,0:T(8,128)(2,1)S(1)}) custom-call(s32[8]{0:T(128)} %table.1, s32[1]{0:T(128)S(6)} %copy.11.step, bf16[32,240]{1,0:T(8,128)(2,1)} %bitcast.1, bf16[960,1536]{1,0:T(8,128)(2,1)} %ctx_hbm.1, f32[1,4,1536]{2,1,0:T(4,128)} %master_hbm.1, ...), custom_call_target="tpu_custom_call" | custom-call | flops 94371840 | bytes 2949120 | tf_op jit(solution)/shard_map/pallas_call | solution.py:255
  18.2 0.0 copy-done
  18.3 1.2 %shard_map.103 = (f32[1,4,1536]{2,1,0:T(4,128)}, f32[1,4,1536]{2,1,0:T(4,128)}, f32[1,4,1536]{2,1,0:T(4,128)}, bf16[32,1536]{1,0:T(8,128)(2,1)}) custom-call(s32[8]{0:T(128)S(1)} %copy-done, f32[1,4,1536]{2,1,0:T(4,128)S(1)} %get-tuple-element.8.master, f32[1,4,1536]{2,1,0:T(4,128)S(1)} %get-tuple-element.9.first, ...), custom_call_target="tpu_custom_call" | custom-call | tf_op jit(solution)/shard_map/pallas_call | solution.py:289
Async XLA Ops:
  0.6 17.6 %copy-start = (s32[8]{0:T(128)S(1)}, s32[8]{0:T(128)}, u32[]{:S(2)}) copy-start(s32[8]{0:T(128)} %table.1) | copy-start | bytes 100

commit v4 on v3

--- a/solution.py
+++ b/solution.py
@@ -52,7 +52,7 @@
         pl.semaphore_signal(barrier, inc=1, device_id={"dp": flipped(me, k, owners)})
 
     each(1, ranks, lambda k: greet_rank(ranks - k))
-    each(1, owners, greet_owner)
+    each(1, owners, lambda k: greet_owner(owners - k))
 
     table_copy = pltpu.make_async_copy(table_hbm, table, table_sem)
     table_copy.start()

time: 19.7 us -> 19.6 us (level)
  no operation moved by 1% of the time
where the time goes in v4:
time: 19.6 us; the launch traced here: 19.5 us
  Pallas kernels  18.1 us (92%)
  between operations  1.32 us (7%)
    pallas_call x1, Pallas kernels, shards(): pl.pallas_call(functools.partial(kernel, owners, ranks, buckets, width),...  16.9 us
    pallas_call x1, Pallas kernels, shards(): pl.pallas_call(functools.partial(finish_kernel, buckets, width), out_shap...  1.25 us

profile of v4, /device:TPU:0, one launch (start us, length us, event | category | flops | bytes accessed | tf_op | source)
XLA Modules:
  0.0 19.5 jit_solution(18275308687771109654)
XLA Ops:
  0.6 0.0 copy-start
  1.3 16.9 %shard_map.102 = (f32[1,4,1536]{2,1,0:T(4,128)S(1)}, f32[1,4,1536]{2,1,0:T(4,128)S(1)}, f32[1,4,1536]{2,1,0:T(4,128)S(1)}, bf16[8,16,384]{2,1,0:T(8,128)(2,1)S(1)}) custom-call(s32[8]{0:T(128)} %table.1, s32[1]{0:T(128)S(6)} %copy.11.step, bf16[32,240]{1,0:T(8,128)(2,1)} %bitcast.1, bf16[960,1536]{1,0:T(8,128)(2,1)} %ctx_hbm.1, f32[1,4,1536]{2,1,0:T(4,128)} %master_hbm.1, ...), custom_call_target="tpu_custom_call" | custom-call | flops 94371840 | bytes 2949120 | tf_op jit(solution)/shard_map/pallas_call | solution.py:255
  18.2 0.0 copy-done
  18.2 1.2 %shard_map.103 = (f32[1,4,1536]{2,1,0:T(4,128)}, f32[1,4,1536]{2,1,0:T(4,128)}, f32[1,4,1536]{2,1,0:T(4,128)}, bf16[32,1536]{1,0:T(8,128)(2,1)}) custom-call(s32[8]{0:T(128)S(1)} %copy-done, f32[1,4,1536]{2,1,0:T(4,128)S(1)} %get-tuple-element.8.master, f32[1,4,1536]{2,1,0:T(4,128)S(1)} %get-tuple-element.9.first, ...), custom_call_target="tpu_custom_call" | custom-call | tf_op jit(solution)/shard_map/pallas_call | solution.py:289
Async XLA Ops:
  0.6 17.6 %copy-start = (s32[8]{0:T(128)S(1)}, s32[8]{0:T(128)}, u32[]{:S(2)}) copy-start(s32[8]{0:T(128)} %table.1) | copy-start | bytes 100
